TPU v7x, 32 devices: a whole 2x2x4 slice. The times are simulated.
32 devices in a mesh: groups: 2 (over x), stack: 4 (over y, core), bloch: 4 (over z).
Axes of the slice: x: 2, y: 2, z: 4, core: 2. Of those that a mesh axis runs over, the one named last changes fastest.
Arguments:
- drive: float32 [8, 8, 2, 192, 256], P(('groups', 'bloch'), 'stack'), parts along dimension 0, may hold values from -6 to 6
- positions: int32 [512], P('groups'), parts along dimension 0, may hold values from 0 to 3
- materials: int32 [16], P(('groups', 'stack')), parts along dimension 0, may hold values from 0 to 3
- table: float32 [4, 4, 192, 192], replicated, may hold values from -1 to 1
- thickness: float32 [16], P(('groups', 'stack')), parts along dimension 0, may hold values from 0.25 to 4
- decay: float32 [192], replicated, may hold values from 0.0025 to 2
Outputs:
- up_field: float32 [8, 4, 192, 256], P(('groups', 'bloch'), 'stack'), parts along dimension 0
- down_field: float32 [8, 4, 192, 256], P(('groups', 'bloch'), 'stack'), parts along dimension 0
There are 2 independent parts, one for each index of `groups`. A program takes and returns all parts, laid end to end along the dimension named above; an argument that names none is the same for every part. Nothing has to cross between parts.
All inputs are finite; a program needn't handle non-finite values.
Results may differ from a plain program's by a relative error of at most 0.00013.
Values sent between devices are 32-bit elements; how exact they have to be, the bound alone decides.
A program may use at most 64 MiB of HBM per device.

v0:
```python
import math

import jax
import jax.numpy as jnp
from jax import lax
from jax.sharding import PartitionSpec as P

precise = lax.Precision.HIGHEST


def passed_along(block, axis, distance):
    devices = range(lax.axis_size(axis))
    route = [(i - distance, i) for i in devices if i - distance in devices]
    return lax.ppermute(block, axis, route)


def product(left_side, right_side):
    return jnp.einsum("...ij,...jk->...ik", left_side, right_side, precision=precise)


def cas_rows(row_ids, column_ids, cell_count):
    phases = row_ids[:, None] * column_ids[None, :] % cell_count
    angles = phases.astype(jnp.float32) * (2.0 * math.pi / cell_count)
    return (jnp.cos(angles) + jnp.sin(angles)) / math.sqrt(cell_count)


def inverse_gap(coupling):
    identity = jnp.eye(coupling.shape[-1], dtype=jnp.float32)
    system = identity - coupling
    approx = identity + coupling
    for repeat_index in range(6):
        approx = product(approx, 2.0 * identity - product(system, approx))
    return approx


def full_join(above_part, below_part):
    refl_top_a, trans_down_a, trans_up_a, refl_bot_a, src_up_a, src_down_a = above_part
    refl_top_b, trans_down_b, trans_up_b, refl_bot_b, src_up_b, src_down_b = below_part
    gap_inverse = inverse_gap(product(refl_bot_a, refl_top_b))
    down_inner = product(trans_down_b, gap_inverse)
    reflect_inner = product(refl_top_b, gap_inverse)
    bounce_up = product(refl_bot_a, trans_up_b)
    crossing = product(gap_inverse, src_down_a + product(refl_bot_a, src_up_b))
    return (
        refl_top_a + product(trans_up_a, product(reflect_inner, trans_down_a)),
        product(down_inner, trans_down_a),
        product(trans_up_a, trans_up_b + product(reflect_inner, bounce_up)),
        refl_bot_b + product(down_inner, bounce_up),
        src_up_a + product(trans_up_a, product(refl_top_b, crossing) + src_up_b),
        src_down_b + product(trans_down_b, crossing),
    )


def forward_join(above_part, below_part):
    refl_bot_a, src_down_a = above_part
    refl_top_b, trans_down_b, trans_up_b, refl_bot_b, src_up_b, src_down_b = below_part
    gap_inverse = inverse_gap(product(refl_bot_a, refl_top_b))
    down_inner = product(trans_down_b, gap_inverse)
    new_refl = refl_bot_b + product(down_inner, product(refl_bot_a, trans_up_b))
    new_source = src_down_b + product(down_inner, src_down_a + product(refl_bot_a, src_up_b))
    return (new_refl, new_source)


def backward_join(above_part, below_part):
    refl_top_a, trans_down_a, trans_up_a, refl_bot_a, src_up_a, src_down_a = above_part
    refl_top_b, src_up_b = below_part
    gap_inverse = inverse_gap(product(refl_bot_a, refl_top_b))
    reflect_inner = product(refl_top_b, gap_inverse)
    new_refl = refl_top_a + product(trans_up_a, product(reflect_inner, trans_down_a))
    crossing = product(gap_inverse, src_down_a + product(refl_bot_a, src_up_b))
    new_source = src_up_a + product(trans_up_a, product(refl_top_b, crossing) + src_up_b)
    return (new_refl, new_source)


def crossing_down(above_part, below_part):
    refl_bot_a, src_down_a = above_part
    refl_top_b, src_up_b = below_part
    gap_inverse = inverse_gap(product(refl_bot_a, refl_top_b))
    return product(gap_inverse, src_down_a + product(refl_bot_a, src_up_b))


def shards(drive, positions, materials, table, thickness, decay):
    cells_here = drive.shape[0]
    slab_count = drive.shape[1]
    mode_count = drive.shape[3]
    cell_count = cells_here * lax.axis_size("bloch")
    first_cell = lax.axis_index("bloch") * cells_here
    local_ids = first_cell + jnp.arange(cells_here, dtype=jnp.int32)
    offset = jnp.abs(local_ids[:, None] - positions[None, :])
    offset = jnp.minimum(offset, cell_count - offset)
    envelope = 1.0 / (1.0 + offset.astype(jnp.float32))
    sources = drive * envelope[:, None, None, None, :]
    wave_ids = jnp.arange(lax.axis_size("bloch") * cells_here, dtype=jnp.int32)
    spectrum = lax.psum_scatter(
        jnp.einsum(
            "kc,clsme->klsme", cas_rows(wave_ids, local_ids, cell_count), sources, precision=precise
        ),
        "bloch",
        scatter_dimension=0,
        tiled=True,
    )
    waves = local_ids.astype(jnp.float32)
    rates = decay[None, :] * (1.0 + 0.5 * jnp.cos(waves * (2.0 * math.pi / cell_count)))[:, None]
    onehot = (materials[:, None] == jnp.arange(table.shape[0], dtype=jnp.int32)[None, :]).astype(
        jnp.float32
    )
    chosen = jnp.einsum("ln,njab->ljab", onehot, table, precision=precise)
    damping = jnp.exp(-thickness[:, None, None] * rates[None])
    own_slab = None
    for layer_index in range(slab_count):
        layer_damp = damping[layer_index]
        scaled = (
            layer_damp[:, None, :, None] * chosen[layer_index][None] * layer_damp[:, None, None, :]
        )
        segment = (
            scaled[:, 0],
            scaled[:, 1],
            scaled[:, 2],
            scaled[:, 3],
            spectrum[:, layer_index, 0],
            spectrum[:, layer_index, 1],
        )
        own_slab = segment if own_slab is None else full_join(own_slab, segment)
    stack_index = lax.axis_index("stack")
    depth = lax.axis_size("stack")

    def unpack(packed):
        return (packed[..., :mode_count], packed[..., mode_count:])

    def pack(pair):
        return jnp.concatenate([pair[0], pair[1]], axis=-1)

    start_down = pack((own_slab[3], own_slab[5]))

    def pass_down(turn_index, carry):
        outgoing, held_prefix = carry
        arrived = passed_along(outgoing, "stack", 1)
        is_turn = stack_index == turn_index
        held_prefix = jnp.where(is_turn, arrived, held_prefix)
        outgoing = lax.cond(
            is_turn, lambda: pack(forward_join(unpack(arrived), own_slab)), lambda: outgoing
        )
        return (outgoing, held_prefix)

    incl_down, excl_down = lax.fori_loop(
        1, depth, pass_down, (start_down, jnp.zeros_like(start_down))
    )
    start_up = pack((own_slab[0], own_slab[4]))

    def pass_up(turn_index, carry):
        outgoing, held_suffix = carry
        arrived = passed_along(outgoing, "stack", -1)
        is_turn = stack_index == depth - 1 - turn_index
        held_suffix = jnp.where(is_turn, arrived, held_suffix)
        outgoing = lax.cond(
            is_turn, lambda: pack(backward_join(own_slab, unpack(arrived))), lambda: outgoing
        )
        return (outgoing, held_suffix)

    incl_up, excl_up = lax.fori_loop(1, depth, pass_up, (start_up, jnp.zeros_like(start_up)))
    excl_prefix = unpack(excl_down)
    incl_prefix = unpack(incl_down)
    excl_suffix = unpack(excl_up)
    incl_suffix = unpack(incl_up)
    downward_top = crossing_down(excl_prefix, incl_suffix)
    upward = product(incl_suffix[0], downward_top) + incl_suffix[1]
    downward = crossing_down(incl_prefix, excl_suffix)
    fields = jnp.stack([upward, downward], axis=1)
    cell_ids = jnp.arange(lax.axis_size("bloch") * cells_here, dtype=jnp.int32)
    result = lax.psum_scatter(
        jnp.einsum(
            "ck,ksme->csme", cas_rows(cell_ids, local_ids, cell_count), fields, precision=precise
        ),
        "bloch",
        scatter_dimension=0,
        tiled=True,
    )
    return (result[:, 0:1], result[:, 1:2])


def solution(mesh):
    in_specs = (
        P(("groups", "bloch"), "stack", None, None, None),
        P("groups"),
        P(("groups", "stack")),
        P(),
        P(("groups", "stack")),
        P(),
    )
    out_specs = (
        P(("groups", "bloch"), "stack", None, None),
        P(("groups", "bloch"), "stack", None, None),
    )
    return jax.shard_map(shards, mesh=mesh, in_specs=in_specs, out_specs=out_specs, check_vma=False)
```

profile of v0, /device:TPU:13, one launch (start us, length us, event | category | flops | bytes accessed | tf_op | source)
XLA Modules:
  0.0 247.7 jit_solution(13068270712680972411)
XLA Ops:
  7.3 0.8 fusion.115
  8.1 1.2 multiply_bitcast_fusion
  9.4 2.0 broadcast_multiply_fusion
  11.7 4.1 %fusion.41 = f32[2,4,192,192]{3,0,2,1:T(2,128)S(1)} fusion(f32[4,4,192,192]{3,2,1,0:T(8,128)S(1)} %copy-done, s32[2]{0:T(128)S(1)} %copy-done.16), kind=kOutput, calls=%fused_computation.70 | convolution fusion | flops 14155784 | bytes 3538952 | tf_op jit(solution)/shard_map/ln,njab->ljab/dot_general | solution.py:107
  15.8 1.8 fusion.53
  17.5 1.1 fusion.121
  19.0 0.3 select_subtract_fusion.17
  19.7 0.3 select_subtract_fusion.16
  20.3 0.3 select_subtract_fusion.15
  24.0 1.0 convolution_bitcast_fusion.11
  25.4 1.0 convolution_bitcast_fusion.12
  26.4 1.0 fusion.44
  27.7 1.0 fusion.46
  28.7 43.8 %reduce-scatter.3.cloned.1.call-done = f32[1,2,2,192,256]{4,3,2,1,0:T(8,128)} async-done(((f32[4,2,2,192,256]{4,3,2,1,0:T(8,128)}), f32[1,2,2,192,256]{4,3,2,1,0:T(8,128)}) %reduce-scatter.3.cloned.1.call-update) | async-done | bytes 786448 | tf_op jit(solution)/shard_map/reduce_scatter | solution.py:94
  72.5 1.4 convolution_add_fusion.5
  73.9 1.2 fusion.141
  75.2 1.3 fusion.43
  76.5 1.9 pad_maximum_fusion.3
  78.5 1.2 convolution_add_fusion.4
  79.7 1.2 fusion.45
  81.0 1.9 pad_maximum_fusion.2
  82.9 53.4 %while.39 = (s32[]{:T(128)}, f32[1,192,448]{2,1,0:T(8,128)}, f32[1,192,448]{2,1,0:T(8,128)}, s32[]{:T(128)}, f32[1,192,192]{2,1,0:T(8,128)}, /*index=5*/f32[1,19...) while((s32[]{:T(128)}, f32[1,192,448]{2,1,0:T(8,128)}, ...), condition=%wide.region_8.9_spmd.clone, body=%wide.region_5.8_spmd.clone.sunk | while | flops 1587388416 | bytes 14549358 | solution.py:145
  82.9 1.3 collective-permute-start.1
  84.2 2.6 %collective-permute-done.1 = f32[1,192,448]{2,1,0:T(8,128)S(1)} collective-permute-done((f32[1,192,448]{2,1,0:T(8,128)}, f32[1,192,448]{2,1,0:T(8,128)S(1)}, u32[]{:S(2)}, u32[]{:S(2)}) %collective-permute-start.1) | collective-permute-done | bytes 344096 | tf_op jit(solution)/shard_map/while/body/eval_jaxpr/ppermute | solution.py:14
  86.8 0.8 select_select_fusion.5
  87.7 1.3 collective-permute-start.1
  89.0 8.0 %collective-permute-done.1 = f32[1,192,448]{2,1,0:T(8,128)S(1)} collective-permute-done((f32[1,192,448]{2,1,0:T(8,128)}, f32[1,192,448]{2,1,0:T(8,128)S(1)}, u32[]{:S(2)}, u32[]{:S(2)}) %collective-permute-start.1) | collective-permute-done | bytes 344096 | tf_op jit(solution)/shard_map/while/body/eval_jaxpr/ppermute | solution.py:14
  97.0 1.8 select_select_fusion.5
  98.8 1.3 collective-permute-start.1
  100.1 24.8 %collective-permute-done.1 = f32[1,192,448]{2,1,0:T(8,128)S(1)} collective-permute-done((f32[1,192,448]{2,1,0:T(8,128)}, f32[1,192,448]{2,1,0:T(8,128)S(1)}, u32[]{:S(2)}, u32[]{:S(2)}) %collective-permute-start.1) | collective-permute-done | bytes 344096 | tf_op jit(solution)/shard_map/while/body/eval_jaxpr/ppermute | solution.py:14
  124.9 9.6 %conditional.7 = (f32[1,192,448]{2,1,0:T(8,128)}) conditional(s32[]{:T(128)} %convert_element_type.142, f32[1,192,448]{2,1,0:T(8,128)} %get-tuple-element.702, (f32[1,192,448]{2,1,0:T(8,128)S(1)}, f32[1,192,192]{2,1,0:T(8,128)}, f32[1,192,192]{2,1,0:T(8,128)}, f32[1,192,192]{2,1,0:T(8,128)}, f32[1,192,192]{2,1,0:T(8,128)}, ...), branch_computations={%region_6.6_spmd, %region_7.7_spmd} | conditional | flops 1587216384 | bytes 12140664 | solution.py:140
  124.9 1.2 fusion.32
  126.1 0.3 convolution_subtract_fusion.11
  126.8 0.3 convolution_subtract_fusion.10
  130.2 0.6 fusion.30
  131.1 1.5 fusion.23
  133.0 0.6 fusion.26
  133.6 0.9 pad_maximum_fusion.1
  134.5 1.8 select_select_fusion.5
  136.3 30.4 %while.38 = (s32[]{:T(128)}, f32[1,192,448]{2,1,0:T(8,128)}, f32[1,192,448]{2,1,0:T(8,128)}, s32[]{:T(128)}, f32[1,192,192]{2,1,0:T(8,128)}, /*index=5*/f32[1,19...) while((s32[]{:T(128)}, f32[1,192,448]{2,1,0:T(8,128)}, ...), condition=%wide.region_4.5_spmd.clone, body=%wide.region_1.4_spmd.clone.sunk | while | flops 1813929984 | bytes 15827330 | solution.py:160
  136.3 1.3 collective-permute-start
  137.6 1.5 collective-permute-done
  139.1 0.8 select_select_fusion.4
  140.0 14.0 %collective-permute-start = (f32[1,192,448]{2,1,0:T(8,128)}, f32[1,192,448]{2,1,0:T(8,128)S(1)}, u32[]{:S(2)}, u32[]{:S(2)}) collective-permute-start(f32[1,192,448]{2,1,0:T(8,128)} %get-tuple-element.664), channel_id=1, source_target_pairs={{4,0},{8,4},{12,8},{5,1},{9,5},{13,9},{6,2},{10,6},{14,10},{7,3},{... | collective-permute-start | bytes 1032200 | tf_op jit(solution)/shard_map/while/body/eval_jaxpr/ppermute | solution.py:14
  154.0 1.5 collective-permute-done
  155.5 1.8 select_select_fusion.4
  157.3 6.0 %collective-permute-start = (f32[1,192,448]{2,1,0:T(8,128)}, f32[1,192,448]{2,1,0:T(8,128)S(1)}, u32[]{:S(2)}, u32[]{:S(2)}) collective-permute-start(f32[1,192,448]{2,1,0:T(8,128)} %get-tuple-element.664), channel_id=1, source_target_pairs={{4,0},{8,4},{12,8},{5,1},{9,5},{13,9},{6,2},{10,6},{14,10},{7,3},{... | collective-permute-start | bytes 1032200 | tf_op jit(solution)/shard_map/while/body/eval_jaxpr/ppermute | solution.py:14
  163.3 1.5 collective-permute-done
  164.8 1.8 select_select_fusion.4
  166.7 1.6 fusion.48
  168.2 1.3 fusion.81
  169.6 1.6 fusion.52
  171.1 1.3 fusion.75
  172.5 0.3 select_subtract_fusion.11
  173.2 0.3 select_subtract_fusion.10
  173.9 0.3 select_subtract_fusion.9
  174.5 0.3 select_subtract_fusion.8
  177.2 0.3 select_subtract_fusion.5
  177.9 0.3 select_subtract_fusion.4
  178.5 0.3 select_subtract_fusion.3
  180.5 0.3 select_subtract_fusion
  181.6 1.4 broadcast_multiply_fusion.1
  183.0 56.1 %reduce-scatter.5.cloned.1.call-done = f32[1,2,192,256]{3,2,1,0:T(8,128)} async-done(((f32[4,2,192,256]{3,2,1,0:T(8,128)}), f32[1,2,192,256]{3,2,1,0:T(8,128)}) %reduce-scatter.5.cloned.1.call-update) | async-done | bytes 393232 | tf_op jit(solution)/shard_map/reduce_scatter | solution.py:170
  239.0 1.8 fusion.123
  (91 shorter events, 15.2 us)
Async XLA Ops:
  7.2 4.5 %copy-start = (f32[4,4,192,192]{3,2,1,0:T(8,128)S(1)}, f32[4,4,192,192]{3,2,1,0:T(8,128)}, u32[]{:S(2)}) copy-start(f32[4,4,192,192]{3,2,1,0:T(8,128)} %param.17) | copy-start | bytes 7077892
  7.2 65.3 %reduce-scatter.3.cloned.1.call-start = ((), (), s32[]{:S(2)}) async-start(), calls=%async_computation.2 | async-start | bytes 3932160 | tf_op jit(solution)/shard_map/reduce_scatter | solution.py:94
  9.3 2.2 copy-start.17
  9.3 2.2 copy-start.15
  9.3 2.3 copy-start.16
  11.4 227.7 %reduce-scatter.5.cloned.1.call-start = ((), (), s32[]{:S(2)}) async-start(), calls=%async_computation.3 | async-start | bytes 1966080 | tf_op jit(solution)/shard_map/reduce_scatter | solution.py:170
  18.6 4.4 %copy-start.11 = (f32[1,1,192,192]{3,0,2,1:T(1,128)}, f32[1,1,192,192]{3,0,2,1:T(1,128)S(1)}, u32[]{:S(2)}) copy-start(f32[1,1,192,192]{3,0,2,1:T(1,128)S(1)} %get-tuple-element.525) | copy-start | bytes 442372
  18.6 6.4 %copy-start.14 = (f32[1,1,192,192]{3,0,2,1:T(1,128)}, f32[1,1,192,192]{3,0,2,1:T(1,128)S(1)}, u32[]{:S(2)}) copy-start(f32[1,1,192,192]{3,0,2,1:T(1,128)S(1)} %get-tuple-element.514) | copy-start | bytes 442372
  23.0 2.0 copy-start.12
  76.5 6.3 %copy-start.3 = (f32[1,192,256]{2,1,0:T(8,128)}, f32[1,192,256]{2,1,0:T(8,128)S(1)}, u32[]{:S(2)}) copy-start(f32[1,192,256]{2,1,0:T(8,128)S(1)} %fusion.43) | copy-start | bytes 589828
  81.0 1.9 copy-start.6
  82.9 3.9 %collective-permute-start.1 = (f32[1,192,448]{2,1,0:T(8,128)}, f32[1,192,448]{2,1,0:T(8,128)S(1)}, u32[]{:S(2)}, u32[]{:S(2)}) collective-permute-start(f32[1,192,448]{2,1,0:T(8,128)} %get-tuple-element.702), channel_id=1, source_target_pairs={{0,4},{4,8},{8,12},{1,5},{5,9},{9,13},{2,6},{6,10},{10,14},{3,7},{... | collective-permute-start | bytes 1032200 | tf_op jit(solution)/shard_map/while/body/eval_jaxpr/ppermute | solution.py:14
  87.7 9.3 %collective-permute-start.1 = (f32[1,192,448]{2,1,0:T(8,128)}, f32[1,192,448]{2,1,0:T(8,128)S(1)}, u32[]{:S(2)}, u32[]{:S(2)}) collective-permute-start(f32[1,192,448]{2,1,0:T(8,128)} %get-tuple-element.702), channel_id=1, source_target_pairs={{0,4},{4,8},{8,12},{1,5},{5,9},{9,13},{2,6},{6,10},{10,14},{3,7},{... | collective-permute-start | bytes 1032200 | tf_op jit(solution)/shard_map/while/body/eval_jaxpr/ppermute | solution.py:14
  98.8 26.1 %collective-permute-start.1 = (f32[1,192,448]{2,1,0:T(8,128)}, f32[1,192,448]{2,1,0:T(8,128)S(1)}, u32[]{:S(2)}, u32[]{:S(2)}) collective-permute-start(f32[1,192,448]{2,1,0:T(8,128)} %get-tuple-element.702), channel_id=1, source_target_pairs={{0,4},{4,8},{8,12},{1,5},{5,9},{9,13},{2,6},{6,10},{10,14},{3,7},{... | collective-permute-start | bytes 1032200 | tf_op jit(solution)/shard_map/while/body/eval_jaxpr/ppermute | solution.py:14
  126.5 3.7 %copy-start.9 = (f32[1,192,192]{2,1,0:T(8,128)S(1)}, f32[1,192,192]{2,1,0:T(8,128)}, u32[]{:S(2)}) copy-start(f32[1,192,192]{2,1,0:T(8,128)} %get-tuple-element.379) | copy-start | bytes 442372 | tf_op jit(solution)/shard_map/while/body/eval_jaxpr/cond
  126.8 3.9 %copy-start.1 = (f32[1,192,192]{2,1,0:T(8,128)S(1)}, f32[1,192,192]{2,1,0:T(8,128)}, u32[]{:S(2)}) copy-start(f32[1,192,192]{2,1,0:T(8,128)} %get-tuple-element.380) | copy-start | bytes 442372 | tf_op jit(solution)/shard_map/while/body/eval_jaxpr/cond
  127.8 4.8 %copy-start.7 = (f32[1,192,256]{2,1,0:T(8,128)S(1)}, f32[1,192,256]{2,1,0:T(8,128)}, u32[]{:S(2)}) copy-start(f32[1,192,256]{2,1,0:T(8,128)} %get-tuple-element.382) | copy-start | bytes 589828 | tf_op jit(solution)/shard_map/while/body/eval_jaxpr/cond
  128.2 4.8 %copy-start.4 = (f32[1,192,256]{2,1,0:T(8,128)S(1)}, f32[1,192,256]{2,1,0:T(8,128)}, u32[]{:S(2)}) copy-start(f32[1,192,256]{2,1,0:T(8,128)} %get-tuple-element.381) | copy-start | bytes 589828 | tf_op jit(solution)/shard_map/while/body/eval_jaxpr/cond
  136.3 2.8 %collective-permute-start = (f32[1,192,448]{2,1,0:T(8,128)}, f32[1,192,448]{2,1,0:T(8,128)S(1)}, u32[]{:S(2)}, u32[]{:S(2)}) collective-permute-start(f32[1,192,448]{2,1,0:T(8,128)} %get-tuple-element.664), channel_id=1, source_target_pairs={{4,0},{8,4},{12,8},{5,1},{9,5},{13,9},{6,2},{10,6},{14,10},{7,3},{... | collective-permute-start | bytes 1032200 | tf_op jit(solution)/shard_map/while/body/eval_jaxpr/ppermute | solution.py:14
  140.0 15.6 %collective-permute-start = (f32[1,192,448]{2,1,0:T(8,128)}, f32[1,192,448]{2,1,0:T(8,128)S(1)}, u32[]{:S(2)}, u32[]{:S(2)}) collective-permute-start(f32[1,192,448]{2,1,0:T(8,128)} %get-tuple-element.664), channel_id=1, source_target_pairs={{4,0},{8,4},{12,8},{5,1},{9,5},{13,9},{6,2},{10,6},{14,10},{7,3},{... | collective-permute-start | bytes 1032200 | tf_op jit(solution)/shard_map/while/body/eval_jaxpr/ppermute | solution.py:14
  157.3 7.5 %collective-permute-start = (f32[1,192,448]{2,1,0:T(8,128)}, f32[1,192,448]{2,1,0:T(8,128)S(1)}, u32[]{:S(2)}, u32[]{:S(2)}) collective-permute-start(f32[1,192,448]{2,1,0:T(8,128)} %get-tuple-element.664), channel_id=1, source_target_pairs={{4,0},{8,4},{12,8},{5,1},{9,5},{13,9},{6,2},{10,6},{14,10},{7,3},{... | collective-permute-start | bytes 1032200 | tf_op jit(solution)/shard_map/while/body/eval_jaxpr/ppermute | solution.py:14
  173.2 3.7 %copy-start.13 = (f32[1,192,448]{2,1,0:T(8,128)S(1)}, f32[1,192,448]{2,1,0:T(8,128)}, u32[]{:S(2)}) copy-start(f32[1,192,448]{2,1,0:T(8,128)} %get-tuple-element.400) | copy-start | bytes 1032196
Sparse Core Ops, SparseCore 0:
  11.5 60.9 reduce-scatter.2
  183.1 55.8 reduce-scatter.4
where the time goes:
time: 252 us; the launch traced here: 248 us
  waiting for transfers between devices  140 us (56%)
  matrix products  43.5 us (17%)
  starting transfers between devices  25.2 us (10%)
  other arithmetic  21.1 us (8%)
  between operations  14.8 us (6%)
  local copies, waits for them, and re-layouts  2.96 us (1%)
    reduce_scatter x1, waiting for transfers between devices, shards(): lax.psum_scatter(jnp.einsum('ck,ksme->csme', cas_rows(cell_ids, local_ids...  56.1 us
    reduce_scatter x1, waiting for transfers between devices, shards(): lax.psum_scatter(jnp.einsum('kc,clsme->klsme', cas_rows(wave_ids, local_i...  43.8 us
    ppermute x6, waiting for transfers between devices, passed_along(): return lax.ppermute(block, axis, route)  39.9 us
    dot_general x76, matrix products, product(): jnp.einsum('...ij,...jk->...ik', left_side, right_side, precision=precise)  39.5 us
    ppermute x6, starting transfers between devices, passed_along(): return lax.ppermute(block, axis, route)  25.2 us
  transfers between devices with their start and end apart: 8, of which 8 were waited for; matrix products, arithmetic and copies ran while one was open for 7% of the time, Pallas kernels for 0%

commit v1 on v0

v1 whole, which is shorter than its diff:
```python
import functools
import math

import jax
import jax.numpy as jnp
from jax import lax
from jax.experimental import pallas as pl
from jax.experimental.pallas import tpu as pltpu
from jax.sharding import PartitionSpec as P

MESH = pl.DeviceIdType.MESH
f32 = jnp.float32
bf16 = jnp.bfloat16
R_IN, T_UP, GAP, D_DOWN, Q_BOT, R_D = range(6)


def split(value):
    high = value.astype(bf16)
    return high, (value - high.astype(f32)).astype(bf16)


def mm(left, right):
    return jnp.dot(left, right, preferred_element_type=f32)


def mm3(left, right):
    return mm(left[0], right[0]) + (mm(left[0], right[1]) + mm(left[1], right[0]))


def cas(row, column, count):
    angle = 2.0 * math.pi * (row * column % count) / count
    return (math.cos(angle) + math.sin(angle)) / math.sqrt(count)


def gap_series(couplings):
    rows = couplings[0].shape[0]
    splits = [split(c) for c in couplings]
    powers = [s[0] for s in splits]
    sums = list(couplings)
    squares = [mm(p, p) for p in powers]
    for step in range(5):
        powers = [s.astype(bf16) for s in squares]
        if step < 4:
            both = [
                mm(jnp.concatenate([e.astype(bf16), p], axis=0), p) for e, p in zip(sums, powers)
            ]
            sums = [e + s + b[:rows] for e, s, b in zip(sums, squares, both)]
            squares = [b[rows:] for b in both]
        else:
            last = [mm(e.astype(bf16), p) for e, p in zip(sums, powers)]
            sums = [e + s + b for e, s, b in zip(sums, squares, last)]
    parts = [split(e) for e in sums]
    rests = [c + mm3(cs, es) - e for c, cs, es, e in zip(couplings, splits, parts, sums)]
    return [e + r + mm(es[0], r.astype(bf16)) for e, r, es in zip(sums, rests, parts)]


def kernel(
    cells,
    depth,
    packed_ref,
    params_ref,
    table_ref,
    decay_row_ref,
    decay_col_ref,
    out_ref,
    params_all,
    drive_in,
    refl,
    held_high,
    held_low,
    u_send,
    u_in,
    x_send,
    x_in,
    field_send,
    field_in,
    params_sems,
    drive_sems,
    hop_sems,
    field_sems,
):
    slab_layers = packed_ref.shape[1]
    materials = table_ref.shape[0]
    lanes = packed_ref.shape[3]
    half = lanes // 2
    layers = depth * slab_layers
    slots = range(cells // 2 + 1)
    bloch = lax.axis_index("bloch")
    stack = lax.axis_index("stack")

    barrier = pltpu.get_barrier_semaphore()
    for j in range(1, cells):
        pl.semaphore_signal(
            barrier, inc=1, device_id={"bloch": lax.rem(bloch + j, cells)}, device_id_type=MESH
        )
    for j in range(1, depth):
        pl.semaphore_signal(
            barrier, inc=1, device_id={"stack": lax.rem(stack + j, depth)}, device_id_type=MESH
        )
    pl.semaphore_wait(barrier, cells + depth - 2)

    params_copies = []
    for j in range(1, depth):
        copy = pltpu.make_async_remote_copy(
            src_ref=params_ref,
            dst_ref=params_all.at[stack],
            send_sem=params_sems.at[0, j],
            recv_sem=params_sems.at[1, j],
            device_id={"stack": lax.rem(stack + j, depth)},
            device_id_type=MESH,
        )
        copy.start()
        params_copies.append(copy)
    drive_copies = []
    for j in range(1, cells):
        peer = lax.rem(bloch + j, cells)
        copy = pltpu.make_async_remote_copy(
            src_ref=packed_ref.at[peer],
            dst_ref=drive_in.at[bloch],
            send_sem=drive_sems.at[0, j],
            recv_sem=drive_sems.at[1, j],
            device_id={"bloch": peer},
            device_id_type=MESH,
        )
        copy.start()
        drive_copies.append(copy)
    params_all[stack] = params_ref[...]
    drive_in[bloch] = packed_ref[bloch]
    refl[...] = jnp.zeros_like(refl)
    for copy in params_copies:
        copy.wait()

    def hold(place, name, slot, value):
        parts = split(value)
        held_high[place, name, slot] = parts[0]
        held_low[place, name, slot] = parts[1]
        return parts

    def layer_step(turn, carry):
        layer = layers - 1 - turn
        place = lax.rem(layer, slab_layers)
        param = params_all[layer // slab_layers, place]
        width = param[0:1, :]
        chosen = []
        for block in range(4):
            total = None
            for n in range(materials):
                weight = jnp.where(param[1:2, :] == float(n), 1.0, 0.0)
                term = table_ref[n, block] * weight
                total = term if total is None else total + term
            chosen.append(total)
        row_rate = width * decay_row_ref[...]
        col_rate = width[:, 0:1] * decay_col_ref[...]
        scaled = []
        for slot in slots:
            factor = 1.0 + 0.5 * math.cos(2.0 * math.pi * slot / cells)
            row = jnp.exp(-row_rate * factor)
            col = jnp.exp(-col_rate * factor)
            scaled.append([col * block * row for block in chosen])
        below = [hold(place, R_IN, q, refl[q]) for q in slots]
        bottom = [hold(place, Q_BOT, q, scaled[q][3]) for q in slots]
        couplings = [mm3(below[q], bottom[q]) for q in slots]
        down = [hold(place, D_DOWN, q, scaled[q][1]) for q in slots]
        below_down = [hold(place, R_D, q, mm3(below[q], down[q])) for q in slots]
        gaps = gap_series(couplings)
        gap_parts = [hold(place, GAP, q, gaps[q]) for q in slots]
        ups = [split(scaled[q][2]) for q in slots]
        lifts = [
            hold(place, T_UP, q, scaled[q][2] + mm3(ups[q], gap_parts[q])) for q in slots
        ]
        for q in slots:
            refl[q] = scaled[q][0] + mm3(lifts[q], below_down[q])
        return carry

    lax.fori_loop(0, layers - slab_layers * stack, layer_step, 0)

    def held(place, name, slot):
        return held_high[place, name, slot], held_low[place, name, slot]

    def apply(place, name, values):
        return [mm3(held(place, name, q), split(values[q])) for q in slots]

    def added(*terms):
        return [functools.reduce(lambda a, b: a + b, group) for group in zip(*terms)]

    lift_all = [held(0, T_UP, q) for q in slots]
    for place in range(1, slab_layers):
        lift_all = [split(mm3(lift_all[q], held(place, T_UP, q))) for q in slots]
    through = None
    for place in range(slab_layers):
        bounce = []
        for q in slots:
            bottom = held(place, Q_BOT, q)
            whole = bottom[0].astype(f32) + bottom[1].astype(f32)
            bounce.append(split(whole + mm3(bottom, held(place, GAP, q))))
        step = []
        for q in slots:
            down = held(place, D_DOWN, q)
            whole = down[0].astype(f32) + down[1].astype(f32)
            step.append(split(whole + mm3(bounce[q], held(place, R_D, q))))
        through = step if through is None else [split(mm3(step[q], through[q])) for q in slots]

    for copy in drive_copies:
        copy.wait()
    lane = lax.broadcasted_iota(jnp.int32, drive_in.shape[2:], 1)
    lower = lane < half
    up_src, down_src = [], []
    for place in range(slab_layers):
        spectrum = []
        for k in range(cells):
            total = None
            for c in range(cells):
                term = drive_in[c, place] * cas(k, c, cells)
                total = term if total is None else total + term
            spectrum.append(total)
        ups, downs = [], []
        for q in slots:
            one, other = spectrum[q], spectrum[(cells - q) % cells]
            ups.append(jnp.where(lower, one, pltpu.roll(other, half, 1)))
            downs.append(jnp.where(lower, pltpu.roll(one, half, 1), other))
        up_src.append(ups)
        down_src.append(downs)

    lit = [apply(place, R_IN, down_src[place]) for place in range(slab_layers)]
    base = None
    for place in reversed(range(slab_layers)):
        inner = lit[place] if base is None else added(lit[place], base)
        base = added(up_src[place], apply(place, T_UP, inner))

    def hop(send_ref, in_ref, which, peer):
        return pltpu.make_async_remote_copy(
            src_ref=send_ref,
            dst_ref=in_ref,
            send_sem=hop_sems.at[0, which],
            recv_sem=hop_sems.at[1, which],
            device_id={"stack": peer},
            device_id_type=MESH,
        )

    hop_up = hop(u_send, u_in, 0, lax.rem(stack + depth - 1, depth))
    hop_down = hop(x_send, x_in, 1, lax.rem(stack + 1, depth))

    @pl.when(stack == depth - 1)
    def _():
        u_in[...] = jnp.zeros_like(u_in)

    @pl.when(stack < depth - 1)
    def _():
        hop_up.wait_recv()

    under = [u_in[q] for q in slots]
    top = added(base, [mm3(lift_all[q], split(under[q])) for q in slots])
    for q in slots:
        u_send[q] = top[q]

    @pl.when(stack > 0)
    def _():
        hop_up.start()

    inner_up = [under]
    for place in reversed(range(1, slab_layers)):
        inner = added(lit[place], inner_up[0])
        inner_up.insert(0, added(up_src[place], apply(place, T_UP, inner)))
    falling = None
    for place in range(slab_layers):
        gone = down_src[place]
        if falling is not None:
            gone = added(gone, apply(place, D_DOWN, falling))
            rise = added(apply(place, R_IN, gone), inner_up[place])
        else:
            rise = added(lit[place], inner_up[place])
        rise = added(rise, apply(place, GAP, rise))
        falling = added(gone, apply(place, Q_BOT, rise))

    @pl.when(stack == 0)
    def _():
        x_in[...] = jnp.zeros_like(x_in)

    @pl.when(stack > 0)
    def _():
        hop_down.wait_recv()

    over = [split(x_in[q]) for q in slots]
    lowest = added(falling, [mm3(through[q], over[q]) for q in slots])
    for q in slots:
        x_send[q] = lowest[q]

    @pl.when(stack < depth - 1)
    def _():
        hop_down.start()

    highest = added(top, [mm3(split(refl[q]), over[q]) for q in slots])
    for c in range(cells):
        rise, fall = None, None
        for q in slots:
            other = (cells - q) % cells
            other_weight = cas(c, other, cells) if other != q else 0.0
            weight = jnp.where(lower, cas(c, q, cells), other_weight)
            rise = highest[q] * weight if rise is None else rise + highest[q] * weight
            fall = lowest[q] * weight if fall is None else fall + lowest[q] * weight
        rise = rise + pltpu.roll(rise, half, 1)
        fall = fall + pltpu.roll(fall, half, 1)
        field_send[c] = jnp.where(lower, rise, fall)
    field_copies = []
    for j in range(1, cells):
        peer = lax.rem(bloch + j, cells)
        copy = pltpu.make_async_remote_copy(
            src_ref=field_send.at[peer],
            dst_ref=field_in.at[bloch],
            send_sem=field_sems.at[0, j],
            recv_sem=field_sems.at[1, j],
            device_id={"bloch": peer},
            device_id_type=MESH,
        )
        copy.start()
        field_copies.append(copy)
    field_in[bloch] = field_send[bloch]

    @pl.when(stack > 0)
    def _():
        hop_up.wait_send()

    @pl.when(stack < depth - 1)
    def _():
        hop_down.wait_send()

    for copy in field_copies:
        copy.wait()
    out_ref[...] = field_in[...]


def shards(drive, positions, materials, table, thickness, decay):
    cells_here, slab_layers, ways, modes, columns = drive.shape
    cells = cells_here * lax.axis_size("bloch")
    depth = lax.axis_size("stack")
    assert cells_here == 1 and ways == 2
    share = columns // cells
    half = max(share, 64)
    offset = jnp.abs(lax.axis_index("bloch") - positions)
    offset = jnp.minimum(offset, cells - offset)
    envelope = 1.0 / (1.0 + offset.astype(f32))
    sources = drive[0] * envelope
    packed = sources.reshape(slab_layers, ways, modes, cells, share)
    packed = jnp.transpose(packed, (3, 0, 2, 1, 4))
    packed = jnp.pad(packed, ((0, 0),) * 4 + ((0, half - share),))
    packed = packed.reshape(cells, slab_layers, modes, ways * half)
    params = jnp.stack([thickness] + [materials.astype(f32)] * 7, axis=1)
    params = jnp.broadcast_to(params[:, :, None], (slab_layers, 8, modes))
    slots = cells // 2 + 1
    lanes = ways * half
    vmem = pl.BlockSpec(memory_space=pltpu.VMEM)
    fields = pl.pallas_call(
        functools.partial(kernel, cells, depth),
        out_shape=jax.ShapeDtypeStruct((cells, modes, lanes), f32),
        in_specs=[vmem] * 5,
        out_specs=vmem,
        scratch_shapes=[
            pltpu.VMEM((depth, slab_layers, 8, modes), f32),
            pltpu.VMEM((cells, slab_layers, modes, lanes), f32),
            pltpu.VMEM((slots, modes, modes), f32),
            pltpu.VMEM((slab_layers, 6, slots, modes, modes), bf16),
            pltpu.VMEM((slab_layers, 6, slots, modes, modes), bf16),
            pltpu.VMEM((slots, modes, lanes), f32),
            pltpu.VMEM((slots, modes, lanes), f32),
            pltpu.VMEM((slots, modes, lanes), f32),
            pltpu.VMEM((slots, modes, lanes), f32),
            pltpu.VMEM((cells, modes, lanes), f32),
            pltpu.VMEM((cells, modes, lanes), f32),
            pltpu.SemaphoreType.DMA((2, depth)),
            pltpu.SemaphoreType.DMA((2, cells)),
            pltpu.SemaphoreType.DMA((2, 2)),
            pltpu.SemaphoreType.DMA((2, cells)),
        ],
        compiler_params=pltpu.CompilerParams(
            collective_id=0, has_side_effects=True, vmem_limit_bytes=48 * 1024 * 1024
        ),
    )(packed, params, table, decay[None, :], decay[:, None])
    fields = fields.reshape(cells, modes, ways, half)[..., :share]
    fields = jnp.transpose(fields, (2, 1, 0, 3)).reshape(ways, 1, 1, modes, columns)
    return (fields[0], fields[1])


def solution(mesh):
    in_specs = (
        P(("groups", "bloch"), "stack", None, None, None),
        P("groups"),
        P(("groups", "stack")),
        P(),
        P(("groups", "stack")),
        P(),
    )
    out_specs = (
        P(("groups", "bloch"), "stack", None, None),
        P(("groups", "bloch"), "stack", None, None),
    )
    return jax.shard_map(shards, mesh=mesh, in_specs=in_specs, out_specs=out_specs, check_vma=False)
```

time: 252 us -> 63 us (0.25); the launches traced: 248 us -> 62.8 us
  waiting for transfers between devices: 140 us -> 0 us
  Pallas kernels: 0 us -> 55.1 us
  matrix products: 43.5 us -> 0 us
  starting transfers between devices: 25.2 us -> 0 us
  other arithmetic: 21.1 us -> 0.86 us
  between operations: 14.8 us -> 0.75 us
  local copies, waits for them, and re-layouts: 2.96 us -> 6.15 us
    reduce_scatter x2 -> x0, waiting for transfers between devices: 99.8 us -> none  [the longest x1 56.1 us: shards(): lax.psum_scatter(jnp.einsum('ck,ksme->csme', cas_rows(cell_ids, local_ids...]
    pallas_call x0 -> x1, Pallas kernels: none -> 55.1 us  [shards(): pl.pallas_call(functools.partial(kernel, cells, depth), out_shape=jax.Sha...]
    dot_general x77 -> x0, matrix products: 43.5 us -> none  [the longest x76 39.5 us: product(): jnp.einsum('...ij,...jk->...ik', left_side, right_side, precision=precise)]
    ppermute x6 -> x0, waiting for transfers between devices: 39.9 us -> none  [passed_along(): return lax.ppermute(block, axis, route)]
    ppermute x6 -> x0, starting transfers between devices: 25.2 us -> none  [passed_along(): return lax.ppermute(block, axis, route)]
    select_n x6 -> x0, other arithmetic: 8.99 us -> none  [the longest x3 4.52 us: pass_down(): held_prefix = jnp.where(is_turn, arrived, held_prefix)]
    unnamed x20 -> x11, local copies, waits for them, and re-layouts: 0.06 us -> 4.96 us
    concatenate x3 -> x0, other arithmetic: 4.72 us -> none  [pack(): return jnp.concatenate([pair[0], pair[1]], axis=-1)]
  transfers between devices with their start and end apart: 8 -> 0, of which waited for: 8 -> 0; matrix products, arithmetic and copies ran while one was open for 7% -> 0% of each run, Pallas kernels for 0% -> 0%
where the time goes in v1:
time: 63 us; the launch traced here: 62.8 us
  Pallas kernels  55.1 us (87%)
  local copies, waits for them, and re-layouts  6.15 us (10%)
  other arithmetic  0.86 us (1%)
  between operations  0.75 us (1%)
    pallas_call x1, Pallas kernels, shards(): pl.pallas_call(functools.partial(kernel, cells, depth), out_shape=jax.Sha...  55.1 us
    unnamed x11, local copies, waits for them, and re-layouts  4.96 us

profile of v1, /device:TPU:13, one launch (start us, length us, event | category | flops | bytes accessed | tf_op | source)
XLA Modules:
  0.0 62.8 jit_solution(13017650494959096020)
XLA Ops:
  0.6 1.5 %copy.20 = f32[1,2,2,192,256]{3,4,2,1,0:T(8,128)S(1)} copy(f32[1,2,2,192,256]{4,3,2,1,0:T(8,128)} %param.6) | data formatting | bytes 1572864 | tf_op args[0]
  2.1 0.0 copy-start.1
  2.1 0.0 copy-start.2
  2.1 0.0 copy-start.3
  2.1 0.7 %fusion.2 = f32[256]{0:T(256)S(1)} fusion(s32[256]{0:T(256)} %param.7, s32[]{:T(128)S(6)} %axis_index.12), kind=kLoop, calls=%fused_computation.4 | loop fusion | flops 1792 | bytes 2052 | tf_op jit(solution)/shard_map/div | solution.py:341
  2.8 0.1 mul.11
  2.9 0.2 multiply_bitcast_fusion
  3.1 0.1 copy.21
  3.2 0.3 copy.30.packed_ref
  3.5 0.0 copy-done.1
  3.5 0.1 copy.31.decay_col_ref
  3.6 0.0 copy-done.2
  3.7 0.1 copy.23
  3.7 0.0 copy-done.3
  3.7 0.1 copy.22
  3.8 0.1 stack.8
  3.9 0.1 broadcast_in_dim.6.params_ref
  4.0 0.0 copy-start
  4.0 1.9 %copy-done = f32[4,4,192,192]{3,2,1,0:T(8,128)S(1)} copy-done((f32[4,4,192,192]{3,2,1,0:T(8,128)S(1)}, f32[4,4,192,192]{3,2,1,0:T(8,128)}, u32[]{:S(2)}) %copy-start) | copy-done | bytes 2359320
  5.9 55.1 %shard_map.77 = f32[4,192,128]{2,1,0:T(8,128)S(1)} custom-call(f32[4,2,192,128]{3,2,1,0:T(8,128)S(1)} %copy.30.packed_ref, f32[2,8,192]{2,1,0:T(8,128)S(1)} %broadcast_in_dim.6.params_ref, f32[4,4,192,192]{3,2,1,0:T(8,128)S(1)} %copy-done, f32[1,192]{1,0:T(1,128)S(1)} %bitcast.15, f32[192,1]{1,0:T(8,128)S(1)} %copy.31.decay_col_ref), custom_call_target="tpu_custom_call" | custom-call | tf_op jit(solution)/shard_map/pallas_call | solution.py:352
  61.0 0.2 copy.32
  61.2 0.8 %copy.33 = f32[1,1,192,256]{3,2,1,0:T(8,128)} copy(f32[1,1,192,256]{2,3,1,0:T(8,128)S(1)} %bitcast.20) | data formatting | bytes 393216
  62.0 0.8 %copy.34 = f32[1,1,192,256]{3,2,1,0:T(8,128)} copy(f32[1,1,192,256]{2,3,1,0:T(8,128)S(1)} %bitcast.19) | data formatting | bytes 393216
  (2 shorter events, 0.0 us)
Async XLA Ops:
  2.1 1.4 %copy-start.1 = (f32[192]{0:T(256)S(1)}, f32[192]{0:T(256)}, u32[]{:S(2)}) copy-start(f32[192]{0:T(256)} %param.11) | copy-start | bytes 2308
  2.1 1.5 %copy-start.2 = (s32[2]{0:T(128)S(1)}, s32[2]{0:T(128)}, u32[]{:S(2)}) copy-start(s32[2]{0:T(128)} %param.8) | copy-start | bytes 28
  2.1 1.6 %copy-start.3 = (f32[2]{0:T(128)S(1)}, f32[2]{0:T(128)}, u32[]{:S(2)}) copy-start(f32[2]{0:T(128)} %param.10) | copy-start | bytes 28
  4.0 1.9 %copy-start = (f32[4,4,192,192]{3,2,1,0:T(8,128)S(1)}, f32[4,4,192,192]{3,2,1,0:T(8,128)}, u32[]{:S(2)}) copy-start(f32[4,4,192,192]{3,2,1,0:T(8,128)} %table_ref.1) | copy-start | bytes 7077892

commit v2 on v1

v2 whole, which is shorter than its diff:
```python
import functools
import math

import jax
import jax.numpy as jnp
from jax import lax
from jax.experimental import pallas as pl
from jax.experimental.pallas import tpu as pltpu
from jax.sharding import PartitionSpec as P

MESH = pl.DeviceIdType.MESH
f32 = jnp.float32
bf16 = jnp.bfloat16
R_IN, T_UP, GAP, D_DOWN, Q_BOT, R_D = range(6)


def split(value):
    high = value.astype(bf16)
    return high, (value - high.astype(f32)).astype(bf16)


def stacked(value):
    return jnp.concatenate(split(value), axis=0)


def mm(left, right):
    return jnp.dot(left, right, preferred_element_type=f32)


def mm3(left, right):
    rows, inner = left.shape[0] // 2, right.shape[0] // 2
    both = mm(left, right[:inner])
    return both[:rows] + (both[rows:] + mm(left[:rows], right[inner:]))


def mm3_columns(left, columns):
    rows, lanes = left.shape[0] // 2, columns.shape[1]
    both = mm(left, jnp.concatenate(split(columns), axis=1))
    cross = both[:rows, lanes:] + both[rows:, :lanes] + both[rows:, lanes:]
    return both[:rows, :lanes] + cross


def cas(row, column, count):
    angle = 2.0 * math.pi * (row * column % count) / count
    return (math.cos(angle) + math.sin(angle)) / math.sqrt(count)


def gap_series(couplings):
    rows = couplings[0].shape[0]
    splits = [stacked(c) for c in couplings]
    powers = [s[:rows] for s in splits]
    sums = list(couplings)
    squares = [mm(p, p) for p in powers]
    for step in range(5):
        powers = [s.astype(bf16) for s in squares]
        if step < 4:
            both = [
                mm(jnp.concatenate([e.astype(bf16), p], axis=0), p) for e, p in zip(sums, powers)
            ]
            sums = [e + s + b[:rows] for e, s, b in zip(sums, squares, both)]
            squares = [b[rows:] for b in both]
        else:
            last = [mm(e.astype(bf16), p) for e, p in zip(sums, powers)]
            sums = [e + s + b for e, s, b in zip(sums, squares, last)]
    parts = [stacked(e) for e in sums]
    rests = [c + mm3(cs, es) - e for c, cs, es, e in zip(couplings, splits, parts, sums)]
    return [e + r + mm(es[:rows], r.astype(bf16)) for e, r, es in zip(sums, rests, parts)]


def kernel(
    cells,
    depth,
    drive_hbm,
    positions_ref,
    thickness_ref,
    materials_ref,
    table_hbm,
    decay_row_ref,
    up_ref,
    down_ref,
    drive_ref,
    table_ref,
    packed_ref,
    params_ref,
    params_all,
    drive_in,
    refl,
    held,
    through,
    u_send,
    u_in,
    x_send,
    x_in,
    field_send,
    field_in,
    load_sems,
    params_sems,
    drive_sems,
    hop_sems,
    field_sems,
):
    slab_layers = packed_ref.shape[1]
    materials = table_ref.shape[0]
    modes = packed_ref.shape[2]
    lanes = packed_ref.shape[3]
    half = lanes // 2
    share = drive_ref.shape[-1] // cells
    layers = depth * slab_layers
    slots = range(cells // 2 + 1)
    groups = range(cells // 2)
    pairs = [(0, cells // 2)] + [(g, cells - g) for g in groups if g > 0]
    bloch = lax.axis_index("bloch")
    stack = lax.axis_index("stack")
    drive_copy = pltpu.make_async_copy(drive_hbm, drive_ref, load_sems.at[0])
    drive_copy.start()
    table_copy = pltpu.make_async_copy(table_hbm, table_ref, load_sems.at[1])
    table_copy.start()

    barrier = pltpu.get_barrier_semaphore()
    for j in range(1, cells):
        pl.semaphore_signal(
            barrier, inc=1, device_id={"bloch": lax.rem(bloch + j, cells)}, device_id_type=MESH
        )
    for j in range(1, depth):
        pl.semaphore_signal(
            barrier, inc=1, device_id={"stack": lax.rem(stack + j, depth)}, device_id_type=MESH
        )
    param_row = lax.broadcasted_iota(jnp.int32, params_ref.shape[1:], 0)
    for place in range(slab_layers):
        material = materials_ref[place].astype(f32)
        params_ref[place] = jnp.where(param_row == 0, thickness_ref[place], material)
    decay_col = jnp.transpose(jnp.broadcast_to(decay_row_ref[...], (128, modes)))[:, 0:1]
    drive_copy.wait()
    offset = jnp.abs(bloch - positions_ref[...])
    offset = jnp.minimum(offset, cells - offset)
    envelope = 1.0 / (1.0 + offset.astype(f32))
    for place in range(slab_layers):
        ways = [drive_ref[0, place, way] * envelope for way in range(2)]
        for c in range(cells):
            pieces = []
            for way in ways:
                pieces.append(way[:, c * share : (c + 1) * share])
                if share < half:
                    pieces.append(jnp.zeros((modes, half - share), f32))
            packed_ref[c, place] = jnp.concatenate(pieces, axis=1)
    pl.semaphore_wait(barrier, cells + depth - 2)

    params_copies = []
    for j in range(1, depth):
        copy = pltpu.make_async_remote_copy(
            src_ref=params_ref,
            dst_ref=params_all.at[stack],
            send_sem=params_sems.at[0, j],
            recv_sem=params_sems.at[1, j],
            device_id={"stack": lax.rem(stack + j, depth)},
            device_id_type=MESH,
        )
        copy.start()
        params_copies.append(copy)
    drive_copies = []
    for j in range(1, cells):
        peer = lax.rem(bloch + j, cells)
        copy = pltpu.make_async_remote_copy(
            src_ref=packed_ref.at[peer],
            dst_ref=drive_in.at[bloch],
            send_sem=drive_sems.at[0, j],
            recv_sem=drive_sems.at[1, j],
            device_id={"bloch": peer},
            device_id_type=MESH,
        )
        copy.start()
        drive_copies.append(copy)
    params_all[stack] = params_ref[...]
    drive_in[bloch] = packed_ref[bloch]
    refl[...] = jnp.zeros_like(refl)
    table_copy.wait()
    for copy in params_copies:
        copy.wait()

    def hold(place, name, slot, value):
        parts = stacked(value)
        held[place, name, slot] = parts
        return parts

    def layer_blocks(turn):
        layer = layers - 1 - turn
        place = lax.rem(layer, slab_layers)
        param = params_all[layer // slab_layers, place]
        width = param[0:1, :]
        chosen = []
        for block in range(4):
            total = None
            for n in range(materials):
                weight = jnp.where(param[1:2, :] == float(n), 1.0, 0.0)
                term = table_ref[n, block] * weight
                total = term if total is None else total + term
            chosen.append(total)
        row_rate = width * decay_row_ref[...]
        col_rate = width[:, 0:1] * decay_col
        scaled = []
        for slot in slots:
            factor = 1.0 + 0.5 * math.cos(2.0 * math.pi * slot / cells)
            row = jnp.exp(-row_rate * factor)
            col = jnp.exp(-col_rate * factor)
            scaled.append([col * block * row for block in chosen])
        down = [hold(place, D_DOWN, q, scaled[q][1]) for q in slots]
        bottom = [hold(place, Q_BOT, q, scaled[q][3]) for q in slots]

        return place, scaled, down, bottom

    place, scaled, down, bottom = layer_blocks(0)
    for q in slots:
        empty = jnp.zeros((2 * modes, modes), bf16)
        held[place, R_IN, q] = empty
        held[place, R_D, q] = empty
        held[place, GAP, q] = empty
        hold(place, T_UP, q, scaled[q][2])
        refl[q] = scaled[q][0]

    def layer_step(turn, carry):
        place, scaled, down, bottom = layer_blocks(turn)
        below = [hold(place, R_IN, q, refl[q]) for q in slots]
        couplings = [mm3(below[q], bottom[q]) for q in slots]
        below_down = [hold(place, R_D, q, mm3(below[q], down[q])) for q in slots]
        gaps = gap_series(couplings)
        gap_parts = [hold(place, GAP, q, gaps[q]) for q in slots]
        ups = [stacked(scaled[q][2]) for q in slots]
        lifts = [hold(place, T_UP, q, scaled[q][2] + mm3(ups[q], gap_parts[q])) for q in slots]
        for q in slots:
            refl[q] = scaled[q][0] + mm3(lifts[q], below_down[q])
        return carry

    lax.fori_loop(1, layers - slab_layers * stack, layer_step, 0)

    lane = lax.broadcasted_iota(jnp.int32, (modes, lanes), 1)
    lower = lane < half

    def act(matrix, group, columns):
        if group > 0:
            return mm3_columns(matrix(group), columns)
        one = mm3_columns(matrix(0), columns)
        return jnp.where(lower, one, mm3_columns(matrix(cells // 2), columns))

    def apply(place, name, values):
        return [act(lambda q: held[place, name, q], g, values[g]) for g in groups]

    def added(*terms):
        return [functools.reduce(lambda a, b: a + b, group) for group in zip(*terms)]

    lift_all = [held[0, T_UP, q] for q in slots]
    for place in range(1, slab_layers):
        lift_all = [stacked(mm3(lift_all[q], held[place, T_UP, q])) for q in slots]

    def whole(place, name, q):
        return held[place, name, q, :modes].astype(f32) + held[place, name, q, modes:].astype(f32)

    @pl.when(stack > 0)
    def _():
        total = None
        for place in range(slab_layers):
            bounce = [
                stacked(whole(place, Q_BOT, q) + mm3(held[place, Q_BOT, q], held[place, GAP, q]))
                for q in slots
            ]
            step = [
                stacked(whole(place, D_DOWN, q) + mm3(bounce[q], held[place, R_D, q]))
                for q in slots
            ]
            total = step if total is None else [stacked(mm3(step[q], total[q])) for q in slots]
        for q in slots:
            through[q] = total[q]

    for copy in drive_copies:
        copy.wait()
    up_src, down_src = [], []
    for place in range(slab_layers):
        spectrum = []
        for k in range(cells):
            total = None
            for c in range(cells):
                term = drive_in[c, place] * cas(k, c, cells)
                total = term if total is None else total + term
            spectrum.append(total)
        ups, downs = [], []
        for first, second in pairs:
            one, other = spectrum[first], spectrum[second]
            ups.append(jnp.where(lower, one, pltpu.roll(other, half, 1)))
            downs.append(jnp.where(lower, pltpu.roll(one, half, 1), other))
        up_src.append(ups)
        down_src.append(downs)

    lit = [apply(place, R_IN, down_src[place]) for place in range(slab_layers)]
    base = None
    for place in reversed(range(slab_layers)):
        inner = lit[place] if base is None else added(lit[place], base)
        base = added(up_src[place], apply(place, T_UP, inner))

    def hop(send_ref, in_ref, which, peer):
        return [
            pltpu.make_async_remote_copy(
                src_ref=send_ref.at[g],
                dst_ref=in_ref.at[g],
                send_sem=hop_sems.at[0, which, g],
                recv_sem=hop_sems.at[1, which, g],
                device_id={"stack": peer},
                device_id_type=MESH,
            )
            for g in groups
        ]

    hop_up = hop(u_send, u_in, 0, lax.rem(stack + depth - 1, depth))
    hop_down = hop(x_send, x_in, 1, lax.rem(stack + 1, depth))

    @pl.when(stack == depth - 1)
    def _():
        u_in[...] = jnp.zeros_like(u_in)

    under, top = [], []
    for g in groups:

        @pl.when(stack < depth - 1)
        def _():
            hop_up[g].wait_recv()

        under.append(u_in[g])
        top.append(base[g] + act(lambda q: lift_all[q], g, under[g]))
        u_send[g] = top[g]

        @pl.when(stack > 0)
        def _():
            hop_up[g].start()

    inner_up = [under]
    for place in reversed(range(1, slab_layers)):
        inner = added(lit[place], inner_up[0])
        inner_up.insert(0, added(up_src[place], apply(place, T_UP, inner)))
    falling = None
    for place in range(slab_layers):
        gone = down_src[place]
        if falling is not None:
            gone = added(gone, apply(place, D_DOWN, falling))
            rise = added(apply(place, R_IN, gone), inner_up[place])
        else:
            rise = added(lit[place], inner_up[place])
        rise = added(rise, apply(place, GAP, rise))
        falling = added(gone, apply(place, Q_BOT, rise))

    @pl.when(stack == 0)
    def _():
        x_in[...] = jnp.zeros_like(x_in)

    lowest = []
    for g in groups:
        x_send[g] = falling[g]

        @pl.when(stack > 0)
        def _():
            hop_down[g].wait_recv()
            x_send[g] = falling[g] + act(lambda q: through[q], g, x_in[g])

        @pl.when(stack < depth - 1)
        def _():
            hop_down[g].start()

        lowest.append(x_send[g])

    refl_parts = [stacked(refl[q]) for q in slots]
    highest = [top[g] + act(lambda q: refl_parts[q], g, x_in[g]) for g in groups]
    for c in range(cells):
        rise, fall = None, None
        for g in groups:
            weight = jnp.where(lower, cas(c, pairs[g][0], cells), cas(c, pairs[g][1], cells))
            rise = highest[g] * weight if rise is None else rise + highest[g] * weight
            fall = lowest[g] * weight if fall is None else fall + lowest[g] * weight
        rise = rise + pltpu.roll(rise, half, 1)
        fall = fall + pltpu.roll(fall, half, 1)
        field_send[c] = jnp.where(lower, rise, fall)
    field_copies = []
    for j in range(1, cells):
        peer = lax.rem(bloch + j, cells)
        copy = pltpu.make_async_remote_copy(
            src_ref=field_send.at[peer],
            dst_ref=field_in.at[bloch],
            send_sem=field_sems.at[0, j],
            recv_sem=field_sems.at[1, j],
            device_id={"bloch": peer},
            device_id_type=MESH,
        )
        copy.start()
        field_copies.append(copy)
    field_in[bloch] = field_send[bloch]

    @pl.when(stack > 0)
    def _():
        for copy in hop_up:
            copy.wait_send()

    @pl.when(stack < depth - 1)
    def _():
        for copy in hop_down:
            copy.wait_send()

    for copy in field_copies:
        copy.wait()
    up_ref[0, 0] = jnp.concatenate([field_in[c, :, :share] for c in range(cells)], axis=1)
    down_ref[0, 0] = jnp.concatenate(
        [field_in[c, :, half : half + share] for c in range(cells)], axis=1
    )


def shards(drive, positions, materials, table, thickness, decay):
    cells_here, slab_layers, ways, modes, columns = drive.shape
    cells = cells_here * lax.axis_size("bloch")
    depth = lax.axis_size("stack")
    assert cells_here == 1 and ways == 2
    share = columns // cells
    half = max(share, 64)
    slots = cells // 2 + 1
    lanes = ways * half
    vmem = pl.BlockSpec(memory_space=pltpu.VMEM)
    smem = pl.BlockSpec(memory_space=pltpu.SMEM)
    anywhere = pl.BlockSpec(memory_space=pl.ANY)
    hop_buffer = pltpu.VMEM((cells // 2, modes, lanes), f32)
    cell_buffer = pltpu.VMEM((cells, modes, lanes), f32)
    field = jax.ShapeDtypeStruct((1, 1, modes, columns), f32)
    up_field, down_field = pl.pallas_call(
        functools.partial(kernel, cells, depth),
        out_shape=(field, field),
        in_specs=[anywhere, vmem, smem, smem, anywhere, vmem],
        out_specs=(vmem, vmem),
        scratch_shapes=[
            pltpu.VMEM(drive.shape, f32),
            pltpu.VMEM(table.shape, f32),
            pltpu.VMEM((cells, slab_layers, modes, lanes), f32),
            pltpu.VMEM((slab_layers, 8, modes), f32),
            pltpu.VMEM((depth, slab_layers, 8, modes), f32),
            pltpu.VMEM((cells, slab_layers, modes, lanes), f32),
            pltpu.VMEM((slots, modes, modes), f32),
            pltpu.VMEM((slab_layers, 6, slots, 2 * modes, modes), bf16),
            pltpu.VMEM((slots, 2 * modes, modes), bf16),
            hop_buffer,
            hop_buffer,
            hop_buffer,
            hop_buffer,
            cell_buffer,
            cell_buffer,
            pltpu.SemaphoreType.DMA((2,)),
            pltpu.SemaphoreType.DMA((2, depth)),
            pltpu.SemaphoreType.DMA((2, cells)),
            pltpu.SemaphoreType.DMA((2, 2, cells // 2)),
            pltpu.SemaphoreType.DMA((2, cells)),
        ],
        compiler_params=pltpu.CompilerParams(
            collective_id=0, has_side_effects=True, vmem_limit_bytes=60 * 1024 * 1024
        ),
    )(drive, positions[None, :], thickness, materials, table, decay[None, :])
    return (up_field, down_field)


def solution(mesh):
    in_specs = (
        P(("groups", "bloch"), "stack", None, None, None),
        P("groups"),
        P(("groups", "stack")),
        P(),
        P(("groups", "stack")),
        P(),
    )
    out_specs = (
        P(("groups", "bloch"), "stack", None, None),
        P(("groups", "bloch"), "stack", None, None),
    )
    return jax.shard_map(shards, mesh=mesh, in_specs=in_specs, out_specs=out_specs, check_vma=False)
```

time: 63 us -> 54.7 us (0.87)
  Pallas kernels: 55.1 us -> 50.7 us
  local copies, waits for them, and re-layouts: 6.15 us -> 3.23 us
  other arithmetic: 0.86 us -> 0 us
    pallas_call x1, Pallas kernels: 55.1 us -> 50.7 us  [shards(): pl.pallas_call(functools.partial(kernel, cells, depth), out_shape=(field,...]
    unnamed x11 -> x2, local copies, waits for them, and re-layouts: 4.96 us -> 3.23 us
    div x1 -> x0, other arithmetic: 0.7 us -> none  [shards(): envelope = 1.0 / (1.0 + offset.astype(f32))]
where the time goes in v2:
time: 54.7 us; the launch traced here: 54.5 us
  Pallas kernels  50.7 us (93%)
  local copies, waits for them, and re-layouts  3.23 us (6%)
  between operations  0.64 us (1%)
    pallas_call x1, Pallas kernels, shards(): pl.pallas_call(functools.partial(kernel, cells, depth), out_shape=(field,...  50.7 us
    unnamed x2, local copies, waits for them, and re-layouts  3.23 us

profile of v2, /device:TPU:13, one launch (start us, length us, event | category | flops | bytes accessed | tf_op | source)
XLA Modules:
  0.0 54.5 jit_solution(13425749115268523380)
XLA Ops:
  0.6 50.7 %shard_map.77 = (f32[1,1,192,256]{3,2,1,0:T(8,128)}, f32[1,1,192,256]{3,2,1,0:T(8,128)}) custom-call(f32[1,2,2,192,256]{4,3,2,1,0:T(8,128)} %drive_hbm.1, s32[1,256]{1,0:T(1,128)} %bitcast.2, f32[2]{0:T(128)} %thickness_ref.1, s32[2]{0:T(128)} %materials_ref.1, f32[4,4,192,192]{3,2,1,0:T(8,128)} %table_hbm.1, f32[1,192]{1,0:T(1,128)} %bitcast.3), custom_call_target="tpu_custom_call" | custom-call | tf_op jit(solution)/shard_map/pallas_call | solution.py:426
  51.3 1.6 %copy.10 = f32[1,1,192,256]{3,2,1,0:T(8,128)} copy(f32[1,1,192,256]{3,2,1,0:T(8,128)} %get-tuple-element.4) | data formatting | bytes 393216
  52.9 1.6 %copy.11 = f32[1,1,192,256]{3,2,1,0:T(8,128)} copy(f32[1,1,192,256]{3,2,1,0:T(8,128)} %get-tuple-element.5) | data formatting | bytes 393216

commit v3 on v2

--- a/solution.py
+++ b/solution.py
@@ -188,12 +188,11 @@
         param = params_all[layer // slab_layers, place]
         width = param[0:1, :]
         chosen = []
+        material = jnp.broadcast_to(param[1:2, :], (modes, modes))
         for block in range(4):
-            total = None
-            for n in range(materials):
-                weight = jnp.where(param[1:2, :] == float(n), 1.0, 0.0)
-                term = table_ref[n, block] * weight
-                total = term if total is None else total + term
+            total = table_ref[0, block]
+            for n in range(1, materials):
+                total = jnp.where(material == float(n), table_ref[n, block], total)
             chosen.append(total)
         row_rate = width * decay_row_ref[...]
         col_rate = width[:, 0:1] * decay_col

time: 54.7 us -> 54 us (0.987)
  Pallas kernels: 50.7 us -> 49.9 us
    pallas_call x1, Pallas kernels: 50.7 us -> 49.9 us  [shards(): pl.pallas_call(functools.partial(kernel, cells, depth), out_shape=(field,...]
where the time goes in v3:
time: 54 us; the launch traced here: 53.8 us
  Pallas kernels  49.9 us (92%)
  local copies, waits for them, and re-layouts  3.23 us (6%)
  between operations  0.64 us (1%)
    pallas_call x1, Pallas kernels, shards(): pl.pallas_call(functools.partial(kernel, cells, depth), out_shape=(field,...  49.9 us
    unnamed x2, local copies, waits for them, and re-layouts  3.23 us

profile of v3, /device:TPU:13, one launch (start us, length us, event | category | flops | bytes accessed | tf_op | source)
XLA Modules:
  0.0 53.8 jit_solution(15257457738279445645)
XLA Ops:
  0.6 49.9 %shard_map.77 = (f32[1,1,192,256]{3,2,1,0:T(8,128)}, f32[1,1,192,256]{3,2,1,0:T(8,128)}) custom-call(f32[1,2,2,192,256]{4,3,2,1,0:T(8,128)} %drive_hbm.1, s32[1,256]{1,0:T(1,128)} %bitcast.2, f32[2]{0:T(128)} %thickness_ref.1, s32[2]{0:T(128)} %materials_ref.1, f32[4,4,192,192]{3,2,1,0:T(8,128)} %table_hbm.1, f32[1,192]{1,0:T(1,128)} %bitcast.3), custom_call_target="tpu_custom_call" | custom-call | tf_op jit(solution)/shard_map/pallas_call | solution.py:425
  50.6 1.6 %copy.10 = f32[1,1,192,256]{3,2,1,0:T(8,128)} copy(f32[1,1,192,256]{3,2,1,0:T(8,128)} %get-tuple-element.4) | data formatting | bytes 393216
  52.2 1.6 %copy.11 = f32[1,1,192,256]{3,2,1,0:T(8,128)} copy(f32[1,1,192,256]{3,2,1,0:T(8,128)} %get-tuple-element.5) | data formatting | bytes 393216
